TPU v7x, 512 devices: a whole 4x8x8 slice. The times are simulated.
512 devices in a mesh: mp: 32 (over z, y_lo), dp: 16 (over x, y_hi, core).
Axes of the slice: x: 4, y: 8 (y_hi: 2, y_lo: 4; y = y_hi * 4 + y_lo), z: 8, core: 2. Of those that a mesh axis runs over, the one named last changes fastest.
Arguments:
- forward_fields: bfloat16 [16, 4, 65536], P(None, None, 'mp'), may hold values from -6 to 6
- adjoint_fields: bfloat16 [64, 4, 65536], P(None, None, 'mp'), may hold values from -6 to 6
- data_rec: int32 [3072], P('dp'), may hold values from 0 to 63
- data_freq: int32 [3072], P('dp'), may hold values from 0 to 15
- data_coef: float32 [3072, 4], P('dp'), may hold values from -6 to 6
- residual_cols: bfloat16 [3072, 256], P('dp'), may hold values from -6 to 6
Outputs:
- data_update: bfloat16 [3072, 256], P('dp')
- model_update: float32 [65536, 256], P(('mp', 'dp'))
All inputs are finite; a program needn't handle non-finite values.
Results may differ from a plain program's by a relative error of at most 0.0075.
Values may be sent and summed in bfloat16 or wider, within the bound.
No kernel may reach another device: no remote copies, remote signals or barrier semaphores. Data moves between devices by JAX's collectives and lax.ppermute only.
A program may use at most 64 MiB of HBM per device.

v0:
```python
import math
import jax
import jax.numpy as jnp
from jax import lax
from jax.sharding import PartitionSpec as P

GRID_COLS = 128
SWEEPS = 2


def with_halo(array, sides, width):
    for axis, dim in sides:
        peers, length = (lax.axis_size(axis), array.shape[dim])
        up = [(i, (i + 1) % peers) for i in range(peers - 1)]
        down = [(j, i) for i, j in up]
        last = lax.slice_in_dim(array, length - width, length, axis=dim)
        leading = lax.slice_in_dim(array, 0, width, axis=dim)
        before = lax.ppermute(last, axis, up)
        after = lax.ppermute(leading, axis, down)
        array = jnp.concatenate([before, array, after], axis=dim)
    return array


def sweep_once(field):
    center = field[:, 1:-1, :]
    sides = jnp.pad(center, ((0, 0), (0, 0), (1, 1)))
    beside_all = field[:, :-2, :] + field[:, 2:, :] + sides[:, :, :-2] + sides[:, :, 2:]
    return center + 0.2 * (beside_all - 4.0 * center)


def per_device(forward_fields, adjoint_fields, data_rec, data_freq, data_coef, residual_cols):
    rows_here = data_rec.shape[0]
    cells_here = forward_fields.shape[2]
    slab_rows = cells_here // GRID_COLS
    slab_count = lax.axis_size("mp")
    block_count = lax.axis_size("dp")
    adjoint = adjoint_fields[data_rec].astype(jnp.float32)
    forward = forward_fields[data_freq].astype(jnp.float32)
    sens = (0.5 * jnp.sum(data_coef[:, :, None] * adjoint * forward, axis=1)).astype(jnp.bfloat16)
    grid = sens.astype(jnp.float32).reshape(rows_here, slab_rows, GRID_COLS)
    for sweep in range(SWEEPS):
        padded = with_halo(grid, (("mp", 1),), 1)
        grid = sweep_once(padded)
    smooth = grid.reshape(rows_here, cells_here).astype(jnp.bfloat16)
    residual_whole = lax.all_gather(residual_cols, "dp", axis=0, tiled=True)
    gram_tile = lax.dot_general(
        smooth,
        lax.all_gather(sens, "dp", axis=0, tiled=True),
        (((1,), (1,)), ((), ())),
        preferred_element_type=jnp.float32,
    )
    partial_value = jnp.dot(
        gram_tile, residual_whole.astype(jnp.float32), precision=lax.Precision.HIGHEST
    )
    gram_prod = lax.psum(partial_value, "mp") / (cells_here * slab_count)
    data_update = (gram_prod + residual_cols.astype(jnp.float32)).astype(jnp.bfloat16)
    summed = lax.psum_scatter(
        lax.dot_general(
            smooth, data_update, (((0,), (0,)), ((), ())), preferred_element_type=jnp.float32
        ),
        "dp",
        scatter_dimension=0,
        tiled=True,
    )
    model_update = summed / math.sqrt(rows_here * block_count)
    return (data_update, model_update)


def solution(mesh):
    in_specs = (
        P(None, None, "mp"),
        P(None, None, "mp"),
        P("dp"),
        P("dp"),
        P("dp", None),
        P("dp", None),
    )
    out_specs = (P("dp", None), P(("mp", "dp"), None))
    return jax.shard_map(
        per_device, mesh=mesh, in_specs=in_specs, out_specs=out_specs, check_vma=False
    )
```

profile of v0, /device:TPU:1, one launch (start us, length us, event | category | flops | bytes accessed | tf_op | source)
XLA Modules:
  0.0 661.7 jit_solution(15564410182115889151)
XLA Ops:
  7.2 0.8 compare_select_fusion.1
  8.7 0.8 copy.8
  9.5 9.6 %gather_fusion = bf16[192,4,2048]{2,1,0:T(4,128)(2,1)} fusion(bf16[64,4,2048]{2,1,0:T(4,128)(2,1)S(1)} %copy-done, s32[1024]{0:T(1024)S(1)} %pad_clamp_fusion.1), kind=kCustom, calls=%fused_computation | custom fusion | bytes 6292224 | tf_op jit(solution)/shard_map/gather | solution.py:37
  19.1 9.7 %gather_fusion.1 = bf16[192,4,2048]{2,1,0:T(4,128)(2,1)} fusion(bf16[16,4,2048]{2,1,0:T(4,128)(2,1)S(1)} %copy-done.1, s32[1024]{0:T(1024)S(1)} %pad_clamp_fusion), kind=kCustom, calls=%fused_computation.1 | custom fusion | bytes 6292224 | tf_op jit(solution)/shard_map/gather | solution.py:38
  28.8 9.7 %multiply_reduce_fusion = f32[192,2048]{1,0:T(8,128)S(1)} fusion(bf16[192,4,2048]{2,1,0:T(4,128)(2,1)} %gather_fusion.1, bf16[192,4,2048]{2,1,0:T(4,128)(2,1)} %gather_fusion, f32[192,4]{1,0:T(8,128)S(1)} %copy.8), kind=kLoop, calls=%fused_computation.2 | loop fusion | flops 7471104 | bytes 7867392 | tf_op jit(solution)/shard_map/reduce_sum | solution.py:39
  38.5 1.2 convert_bitcast_fusion
  39.8 0.7 all-gather.5.cloned.1.call-update
  40.9 4.0 collective-permute-start
  45.0 1.3 collective-permute-start.1
  46.6 5.8 collective-permute-done.1
  52.5 1.3 fusion.4
  53.9 3.8 collective-permute-start.2
  57.7 1.5 collective-permute-start.3
  59.3 7.2 %collective-permute-done.3 = f32[192,1,128]{2,1,0:T(1,128)S(1)} collective-permute-done((f32[192,1,128]{2,1,0:T(1,128)S(1)}, f32[192,1,128]{2,1,0:T(1,128)S(1)}, u32[]{:S(2)}, u32[]{:S(2)}) %collective-permute-start.3) | collective-permute-done | bytes 98336 | tf_op jit(solution)/shard_map/ppermute | solution.py:19
  66.5 1.3 fusion.10
  67.8 128.4 %all-gather.3.cloned.1.call-done = bf16[3072,2048]{1,0:T(8,128)(2,1)} async-done(((bf16[192,2048]{1,0:T(8,128)(2,1)}), bf16[3072,2048]{1,0:T(8,128)(2,1)}) %all-gather.3.cloned.1.call-update) | async-done | bytes 12582928 | tf_op jit(solution)/shard_map/all_gather | solution.py:48
  196.3 10.3 %fusion.15 = f32[192,3072]{1,0:T(8,128)} fusion(bf16[3072,2048]{1,0:T(8,128)(2,1)} %all-gather.3.cloned.1.call-done, bf16[24,8,16,128]{3,2,1,0:T(8,128)(2,1)S(1)} %bitcast.15), kind=kOutput, calls=%fused_computation.28 | convolution fusion | flops 2415919104 | bytes 15728640 | tf_op jit(solution)/shard_map/dot_general | solution.py:46
  206.5 50.8 %all-gather.5.cloned.1.call-done = bf16[3072,256]{1,0:T(8,128)(2,1)} async-done(((bf16[192,256]{1,0:T(8,128)(2,1)}), bf16[3072,256]{1,0:T(8,128)(2,1)}) %all-gather.5.cloned.1.call-update) | async-done | bytes 1572880 | tf_op jit(solution)/shard_map/all_gather | solution.py:45
  257.3 4.0 fusion.21
  261.4 272.9 %all-reduce.4.cloned.1.call-done = f32[192,256]{1,0:T(8,128)} async-done(((f32[192,256]{1,0:T(8,128)}), f32[192,256]{1,0:T(8,128)}) %all-reduce.4.cloned.1.call-update) | async-done | bytes 196624 | tf_op jit(solution)/shard_map/psum | solution.py:55
  534.3 1.0 add_convert_fusion
  535.2 1.8 fusion.13
  537.1 116.5 %reduce-scatter.2.cloned.1.call-done = f32[128,256]{1,0:T(8,128)} async-done(((f32[2048,256]{1,0:T(8,128)}), f32[128,256]{1,0:T(8,128)}) %reduce-scatter.2.cloned.1.call-update) | async-done | bytes 131088 | tf_op jit(solution)/shard_map/reduce_scatter | solution.py:57
  653.6 1.6 broadcast_multiply_fusion
  (23 shorter events, 1.9 us)
Async XLA Ops:
  7.2 2.3 copy-start
  7.2 189.1 %all-gather.3.cloned.1.call-start = ((), (), s32[]{:S(2)}) async-start(), calls=%async_computation.1 | async-start | bytes 13369344 | tf_op jit(solution)/shard_map/all_gather | solution.py:48
  9.5 9.6 %copy-start.1 = (bf16[16,4,2048]{2,1,0:T(4,128)(2,1)S(1)}, bf16[16,4,2048]{2,1,0:T(4,128)(2,1)}, u32[]{:S(2)}) copy-start(bf16[16,4,2048]{2,1,0:T(4,128)(2,1)} %param.6) | copy-start | bytes 786436
  39.7 217.6 %all-gather.5.cloned.1.call-start = ((), (), s32[]{:S(2)}) async-start(), calls=%async_computation.2 | async-start | bytes 1671168 | tf_op jit(solution)/shard_map/all_gather | solution.py:45
  40.5 493.8 %all-reduce.4.cloned.1.call-start = ((), (), s32[]{:S(2)}) async-start(), calls=%async_computation.3 | async-start | bytes 393216 | tf_op jit(solution)/shard_map/psum | solution.py:55
  40.9 5.7 collective-permute-start
  45.0 7.5 %collective-permute-start.1 = (f32[192,1,128]{2,1,0:T(1,128)S(1)}, f32[192,1,128]{2,1,0:T(1,128)S(1)}, u32[]{:S(2)}, u32[]{:S(2)}) collective-permute-start(f32[192,1,128]{2,1,0:T(1,128)S(1)} %get-tuple-element.7), channel_id=1, source_target_pairs={{16,0},{32,16},{48,32},{64,48},{80,64},{96,80},{112,96},{128,112},... | collective-permute-start | bytes 294920 | tf_op jit(solution)/shard_map/ppermute | solution.py:19
  53.9 5.4 collective-permute-start.2
  57.7 8.8 %collective-permute-start.3 = (f32[192,1,128]{2,1,0:T(1,128)S(1)}, f32[192,1,128]{2,1,0:T(1,128)S(1)}, u32[]{:S(2)}, u32[]{:S(2)}) collective-permute-start(f32[192,1,128]{2,1,0:T(1,128)S(1)} %get-tuple-element.5), channel_id=1, source_target_pairs={{16,0},{32,16},{48,32},{64,48},{80,64},{96,80},{112,96},{128,112},... | collective-permute-start | bytes 294920 | tf_op jit(solution)/shard_map/ppermute | solution.py:19
  206.5 327.7 %copy-start.3 = (bf16[192,256]{1,0:T(8,128)(2,1)S(1)}, bf16[192,256]{1,0:T(8,128)(2,1)}, u32[]{:S(2)}) copy-start(bf16[192,256]{1,0:T(8,128)(2,1)} %param.11) | copy-start | bytes 294916
  261.4 392.2 %reduce-scatter.2.cloned.1.call-start = ((), (), s32[]{:S(2)}) async-start(), calls=%async_computation.4 | async-start | bytes 2228224 | tf_op jit(solution)/shard_map/reduce_scatter | solution.py:57
  535.2 1.9 copy-start.2
Sparse Core Ops, SparseCore 0:
  39.8 156.4 all-gather.2
  199.5 57.7 all-gather.4
  261.5 272.7 all-reduce.3
  539.7 113.8 reduce-scatter.1
where the time goes:
time: 662 us
  waiting for transfers between devices  583 us (88%)
  local copies, waits for them, and re-layouts  20.7 us (3%)
  other arithmetic  17.5 us (3%)
  matrix products  16.1 us (2%)
  between operations  13.9 us (2%)
  starting transfers between devices  10.8 us (2%)
    psum x1, waiting for transfers between devices, per_device(): gram_prod = lax.psum(partial_value, 'mp') / (cells_here * slab_count)  273 us
    all_gather x1, waiting for transfers between devices, per_device(): lax.all_gather(sens, 'dp', axis=0, tiled=True)  128 us
    reduce_scatter x1, waiting for transfers between devices, per_device(): lax.psum_scatter(lax.dot_general(smooth, data_update, (((0,), (0,)), ((),...  116 us
    all_gather x1, waiting for transfers between devices, per_device(): residual_whole = lax.all_gather(residual_cols, 'dp', axis=0, tiled=True)  50.8 us
  transfers between devices with their start and end apart: 8, of which 8 were waited for; matrix products, arithmetic and copies ran while one was open for 2% of the time, Pallas kernels for 0%

commit v1 on v0

--- a/solution.py
+++ b/solution.py
@@ -45,7 +45,9 @@
     residual_whole = lax.all_gather(residual_cols, "dp", axis=0, tiled=True)
     gram_tile = lax.dot_general(
         smooth,
-        lax.all_gather(sens, "dp", axis=0, tiled=True),
+        jnp.concatenate(
+            lax.all_to_all(jnp.stack([sens] * lax.axis_size("dp")), "dp", 0, 0), axis=0
+        ),
         (((1,), (1,)), ((), ())),
         preferred_element_type=jnp.float32,
     )

time: 662 us -> 793 us (1.20)
  waiting for transfers between devices: 583 us -> 699 us
  starting transfers between devices: 10.8 us -> 20.3 us
    ppermute x2, waiting for transfers between devices: 0.41 us -> 283 us  [with_halo(): before = lax.ppermute(last, axis, up)]
    all_gather x1 -> x0, waiting for transfers between devices: 128 us -> none  [per_device(): lax.all_gather(sens, 'dp', axis=0, tiled=True)]
    all_gather x1, waiting for transfers between devices: 50.8 us -> 0.01 us  [per_device(): residual_whole = lax.all_gather(residual_cols, 'dp', axis=0, tiled=True)]
    psum x1, waiting for transfers between devices: 273 us -> 294 us  [per_device(): gram_prod = lax.psum(partial_value, 'mp') / (cells_here * slab_count)]
    all_to_all x0 -> x1, starting transfers between devices: none -> 11.6 us  [per_device(): lax.all_to_all(jnp.stack([sens] * lax.axis_size('dp')), 'dp', 0, 0)]
    ppermute x2, waiting for transfers between devices: 13 us -> 3.95 us  [with_halo(): after = lax.ppermute(leading, axis, down)]
  transfers between devices with their start and end apart: 8 -> 8, of which waited for: 8 -> 6; matrix products, arithmetic and copies ran while one was open for 2% -> 2% of each run, Pallas kernels for 0% -> 0%
where the time goes in v1:
time: 793 us; the launch traced here: 792 us
  waiting for transfers between devices  699 us (88%)
  local copies, waits for them, and re-layouts  26.8 us (3%)
  starting transfers between devices  20.3 us (3%)
  other arithmetic  16.5 us (2%)
  matrix products  16.1 us (2%)
  between operations  13.9 us (2%)
    psum x1, waiting for transfers between devices, per_device(): gram_prod = lax.psum(partial_value, 'mp') / (cells_here * slab_count)  294 us
    ppermute x2, waiting for transfers between devices, with_halo(): before = lax.ppermute(last, axis, up)  283 us
    reduce_scatter x1, waiting for transfers between devices, per_device(): lax.psum_scatter(lax.dot_general(smooth, data_update, (((0,), (0,)), ((),...  117 us
  transfers between devices with their start and end apart: 8, of which 6 were waited for; matrix products, arithmetic and copies ran while one was open for 2% of the time, Pallas kernels for 0%

profile of v1, /device:TPU:1, one launch (start us, length us, event | category | flops | bytes accessed | tf_op | source)
XLA Modules:
  0.0 792.4 jit_solution(6061451918921055192)
XLA Ops:
  7.2 0.8 compare_select_fusion.1
  8.0 0.7 compare_select_fusion
  8.6 0.8 copy.8
  9.5 9.6 %gather_fusion = bf16[192,4,2048]{2,1,0:T(4,128)(2,1)} fusion(bf16[64,4,2048]{2,1,0:T(4,128)(2,1)S(1)} %copy-done, s32[1024]{0:T(1024)S(1)} %pad_clamp_fusion.1), kind=kCustom, calls=%fused_computation | custom fusion | bytes 6292224 | tf_op jit(solution)/shard_map/gather | solution.py:37
  19.1 9.7 %gather_fusion.1 = bf16[192,4,2048]{2,1,0:T(4,128)(2,1)} fusion(bf16[16,4,2048]{2,1,0:T(4,128)(2,1)S(1)} %copy-done.1, s32[1024]{0:T(1024)S(1)} %pad_clamp_fusion), kind=kCustom, calls=%fused_computation.1 | custom fusion | bytes 6292224 | tf_op jit(solution)/shard_map/gather | solution.py:38
  28.8 9.7 %multiply_reduce_fusion = f32[192,2048]{1,0:T(8,128)S(1)} fusion(bf16[192,4,2048]{2,1,0:T(4,128)(2,1)} %gather_fusion.1, bf16[192,4,2048]{2,1,0:T(4,128)(2,1)} %gather_fusion, f32[192,4]{1,0:T(8,128)S(1)} %copy.8), kind=kLoop, calls=%fused_computation.2 | loop fusion | flops 7471104 | bytes 7867392 | tf_op jit(solution)/shard_map/reduce_sum | solution.py:39
  38.7 6.1 stack.2
  44.8 11.6 %all-to-all-start = ((bf16[16,192,2048]{2,1,0:T(8,128)(2,1)}), bf16[16,192,2048]{2,1,0:T(8,128)(2,1)}, u32[]{:S(2)}, u32[]{:S(2)}) async-start(bf16[16,192,2048]{2,1,0:T(8,128)(2,1)} %stack.2), calls=%async_computation | async-start | bytes 25165824 | tf_op jit(solution)/shard_map/all_to_all | solution.py:49
  56.4 0.7 all-gather.2.cloned.1.call-update
  57.5 1.8 collective-permute-start
  59.4 1.3 collective-permute-start.1
  60.7 283.3 %collective-permute-done = f32[192,1,128]{2,1,0:T(1,128)S(1)} collective-permute-done((f32[192,1,128]{2,1,0:T(1,128)S(1)}, f32[192,1,128]{2,1,0:T(1,128)S(1)}, u32[]{:S(2)}, u32[]{:S(2)}) %collective-permute-start) | collective-permute-done | bytes 98336 | tf_op jit(solution)/shard_map/ppermute | solution.py:18
  344.2 1.3 fusion.4
  345.7 4.0 collective-permute-start.2
  349.7 1.5 collective-permute-start.3
  351.3 3.7 collective-permute-done.3
  355.0 1.3 fusion.10
  356.4 10.2 %fusion.15 = f32[192,3072]{1,0:T(8,128)} fusion(bf16[3072,2048]{1,0:T(8,128)(2,1)} %bitcast, bf16[24,8,16,128]{3,2,1,0:T(8,128)(2,1)S(1)} %bitcast.16), kind=kOutput, calls=%fused_computation.28 | convolution fusion | flops 2415919104 | bytes 15728640 | tf_op jit(solution)/shard_map/dot_general | solution.py:46
  366.6 4.0 fusion.21
  370.7 294.1 %all-reduce.4.cloned.1.call-done = f32[192,256]{1,0:T(8,128)} async-done(((f32[192,256]{1,0:T(8,128)}), f32[192,256]{1,0:T(8,128)}) %all-reduce.4.cloned.1.call-update) | async-done | bytes 196624 | tf_op jit(solution)/shard_map/psum | solution.py:57
  664.9 1.0 add_convert_fusion
  665.8 1.8 fusion.13
  667.7 116.6 %reduce-scatter.2.cloned.1.call-done = f32[128,256]{1,0:T(8,128)} async-done(((f32[2048,256]{1,0:T(8,128)}), f32[128,256]{1,0:T(8,128)}) %reduce-scatter.2.cloned.1.call-update) | async-done | bytes 131088 | tf_op jit(solution)/shard_map/reduce_scatter | solution.py:59
  784.3 1.6 broadcast_multiply_fusion
  (23 shorter events, 1.3 us)
Async XLA Ops:
  7.2 2.3 copy-start
  9.5 9.6 %copy-start.1 = (bf16[16,4,2048]{2,1,0:T(4,128)(2,1)S(1)}, bf16[16,4,2048]{2,1,0:T(4,128)(2,1)}, u32[]{:S(2)}) copy-start(bf16[16,4,2048]{2,1,0:T(4,128)(2,1)} %param.6) | copy-start | bytes 786436
  44.8 311.6 %all-to-all-start = ((bf16[16,192,2048]{2,1,0:T(8,128)(2,1)}), bf16[16,192,2048]{2,1,0:T(8,128)(2,1)}, u32[]{:S(2)}, u32[]{:S(2)}) async-start(bf16[16,192,2048]{2,1,0:T(8,128)(2,1)} %stack.2), calls=%async_computation | async-start | bytes 25165824 | tf_op jit(solution)/shard_map/all_to_all | solution.py:49
  56.3 310.3 %all-gather.2.cloned.1.call-start = ((), (), s32[]{:S(2)}) async-start(), calls=%async_computation.2 | async-start | bytes 1671168 | tf_op jit(solution)/shard_map/all_gather | solution.py:45
  57.0 607.8 %all-reduce.4.cloned.1.call-start = ((), (), s32[]{:S(2)}) async-start(), calls=%async_computation.3 | async-start | bytes 393216 | tf_op jit(solution)/shard_map/psum | solution.py:57
  57.5 286.5 %collective-permute-start = (f32[192,1,128]{2,1,0:T(1,128)S(1)}, f32[192,1,128]{2,1,0:T(1,128)S(1)}, u32[]{:S(2)}, u32[]{:S(2)}) collective-permute-start(f32[192,1,128]{2,1,0:T(1,128)S(1)} %get-tuple-element.6), channel_id=1, source_target_pairs={{0,16},{16,32},{32,48},{48,64},{64,80},{80,96},{96,112},{112,128},... | collective-permute-start | bytes 294920 | tf_op jit(solution)/shard_map/ppermute | solution.py:18
  59.4 284.8 %collective-permute-start.1 = (f32[192,1,128]{2,1,0:T(1,128)S(1)}, f32[192,1,128]{2,1,0:T(1,128)S(1)}, u32[]{:S(2)}, u32[]{:S(2)}) collective-permute-start(f32[192,1,128]{2,1,0:T(1,128)S(1)} %get-tuple-element.7), channel_id=1, source_target_pairs={{16,0},{32,16},{48,32},{64,48},{80,64},{96,80},{112,96},{128,112},... | collective-permute-start | bytes 294920 | tf_op jit(solution)/shard_map/ppermute | solution.py:19
  345.7 5.6 collective-permute-start.2
  349.7 5.4 collective-permute-start.3
  366.6 298.3 %copy-start.3 = (bf16[192,256]{1,0:T(8,128)(2,1)S(1)}, bf16[192,256]{1,0:T(8,128)(2,1)}, u32[]{:S(2)}) copy-start(bf16[192,256]{1,0:T(8,128)(2,1)} %param.11) | copy-start | bytes 294916
  370.7 413.6 %reduce-scatter.2.cloned.1.call-start = ((), (), s32[]{:S(2)}) async-start(), calls=%async_computation.4 | async-start | bytes 2228224 | tf_op jit(solution)/shard_map/reduce_scatter | solution.py:59
  665.8 1.9 copy-start.2
Sparse Core Ops, SparseCore 0:
  60.4 127.3 all-gather.1
  370.8 294.0 all-reduce.3
  670.4 113.8 reduce-scatter.1
